TPU v7x, 32 devices: a whole 2x2x4 slice. The times are simulated.
32 devices in a mesh: row: 8 (over y, x, core), col: 4 (over z).
Axes of the slice: x: 2, y: 2, z: 4, core: 2. Of those that a mesh axis runs over, the one named last changes fastest.
Arguments:
- flow_state: float32 [6, 64, 64, 512], P(None, 'row', 'col'), may hold values from -6 to 6
- spectral: float32 [64, 64, 512], P('row', 'col'), may hold values from 0.5 to 2
- step_size: float32 [6], replicated, may hold values from 64 to 1024
- fringe_count: int32 [32, 32], P(('row', 'col')), may hold values from 0 to 32, as said below
- donor_base: int32 [32768], P(('row', 'col')), may hold values from 0 to 56830, as said below
- donor_frac: float32 [3, 32768], P(None, ('row', 'col')), may hold values from 0 to 1
- fringe_cell: int32 [32768], P(('row', 'col')), may hold values from 0 to 65535, as said below
Outputs:
- increment: float32 [6, 64, 64, 512], P(None, 'row', 'col')
Inputs may be any that keep to these rules, and one draw needn't show every extreme that they name: `fringe_count`: entry [s, r] is how many fringe cells of device r take values from device s; for every device s, entry [s, (7 s + 3) mod 32] is 32 (so each sender fills all 32 slots of at least one receiver, and each receiver gets 32 from at least one sender); every other entry is 0 or between 16 and 32. `donor_base`: each value is the flat index of a cell whose j, k, l local indices are below 7, 15, 511. `fringe_cell`: the 1024 entries that belong to one receiving device are distinct cells of its block.
All inputs are finite; a program needn't handle non-finite values.
Results may differ from a plain program's by a relative error of at most 0.0003.
Values sent between devices are 32-bit elements; how exact they have to be, the bound alone decides.
A program may use at most 128 MiB of HBM per device.

v0:
```python
import jax
import jax.numpy as jnp
from jax import lax
from jax.sharding import PartitionSpec as P


def with_halo(x, sides, width):
    for axis, dim in sides:
        count, length = (lax.axis_size(axis), x.shape[dim])
        up = [(i, (i + 1) % count) for i in range(count - 1)]
        down = [(j, i) for i, j in up]
        last = lax.slice_in_dim(x, length - width, length, axis=dim)
        initial = lax.slice_in_dim(x, 0, width, axis=dim)
        before = lax.ppermute(last, axis, up)
        after = lax.ppermute(initial, axis, down)
        x = jnp.concatenate([before, x, after], axis=dim)
    return x


def implicit_factor(length, step_rates):
    position = jnp.arange(length)
    second = (
        jnp.where(position[:, None] == position[None, :], -2.0, 0.0)
        + jnp.where(jnp.abs(position[:, None] - position[None, :]) == 1, 1.0, 0.0)
    ).astype(jnp.float32)
    fourth = jnp.dot(second, second, precision=lax.Precision.HIGHEST)
    operator_matrix = -second + 0.25 * fourth
    identity = jnp.eye(length, dtype=jnp.float32)
    return jax.vmap(lambda one_rate: jnp.linalg.cholesky(identity + one_rate * operator_matrix))(
        step_rates
    )


def solve_lines(factors, columns):
    return jax.vmap(
        lambda factor_one, right_side: jax.scipy.linalg.cho_solve((factor_one, True), right_side)
    )(factors, columns)


def interpolate(flat_block, base_index, fraction, k_cells, l_cells):
    total = jnp.zeros((flat_block.shape[0], base_index.shape[0]), jnp.float32)
    for shift_j in (0, 1):
        for shift_k in (0, 1):
            for shift_l in (0, 1):
                weight_j = fraction[0] if shift_j else 1.0 - fraction[0]
                weight_k = fraction[1] if shift_k else 1.0 - fraction[1]
                weight_l = fraction[2] if shift_l else 1.0 - fraction[2]
                weight = weight_j * weight_k * weight_l
                picked = flat_block[
                    :, base_index + shift_j * k_cells * l_cells + shift_k * l_cells + shift_l
                ]
                total = total + weight[None, :] * picked
    return total


def local(flow_state, spectral, step_size, fringe_count, donor_base, donor_frac, fringe_cell):
    variables, block_j, block_k, block_l = flow_state.shape
    rows_count = lax.axis_size("row")
    cols_count = lax.axis_size("col")
    devices_all = rows_count * cols_count
    slot_total = donor_base.shape[0]
    capacity = slot_total // devices_all
    flat_block = flow_state.reshape(variables, block_j * block_k * block_l)
    outgoing = interpolate(flat_block, donor_base, donor_frac, block_k, block_l)
    arrived, arrived_count = (
        lax.all_to_all(outgoing, ("row", "col"), split_axis=1, concat_axis=1, tiled=True),
        lax.all_to_all(fringe_count, ("row", "col"), split_axis=1, concat_axis=1, tiled=True),
    )
    repeated = jnp.repeat(arrived_count.reshape(-1), capacity)
    position = jnp.arange(slot_total, dtype=jnp.int32) % capacity
    alive = position < repeated
    current = flat_block[:, fringe_cell]
    flat_block = flat_block.at[:, fringe_cell].set(jnp.where(alive[None, :], arrived, current))
    filled = flat_block.reshape(variables, block_j, block_k, block_l)
    padded = with_halo(filled, (("row", 1), ("col", 2)), 1)
    zero_plane = jnp.zeros((variables, block_j, block_k, 1), jnp.float32)
    plus_l = jnp.concatenate([filled[:, :, :, 1:], zero_plane], axis=3)
    minus_l = jnp.concatenate([zero_plane, filled[:, :, :, :-1]], axis=3)
    laplace = (
        padded[:, 2:, 1:-1, :]
        + padded[:, :-2, 1:-1, :]
        + padded[:, 1:-1, 2:, :]
        + padded[:, 1:-1, :-2, :]
        + plus_l
        + minus_l
        - 6.0 * filled
    )
    update = step_size[:, None, None, None] * (spectral[None] * laplace)
    grid_j = block_j * rows_count
    grid_k = block_k * cols_count
    factors_l = implicit_factor(block_l, step_size)
    factors_j = implicit_factor(grid_j, step_size)
    factors_k = implicit_factor(grid_k, step_size)
    moved = update.reshape(variables, block_j * block_k, block_l).transpose(0, 2, 1)
    along_l = (
        solve_lines(factors_l, moved)
        .transpose(0, 2, 1)
        .reshape(variables, block_j, block_k, block_l)
    )
    j_lines = lax.all_to_all(along_l, "row", split_axis=2, concat_axis=1, tiled=True)
    j_shape = j_lines.shape
    solved_j = solve_lines(factors_j, j_lines.reshape(variables, grid_j, -1)).reshape(j_shape)
    along_j = lax.all_to_all(solved_j, "row", split_axis=1, concat_axis=2, tiled=True)
    k_lines = lax.all_to_all(along_j, "col", split_axis=1, concat_axis=2, tiled=True)
    k_shape = k_lines.shape
    k_columns = k_lines.transpose(0, 2, 1, 3).reshape(variables, grid_k, -1)
    solved_k = (
        solve_lines(factors_k, k_columns)
        .reshape(variables, grid_k, k_shape[1], block_l)
        .transpose(0, 2, 1, 3)
    )
    result = lax.all_to_all(solved_k, "col", split_axis=2, concat_axis=1, tiled=True)
    return result


def solution(mesh):
    placed = (
        P(None, "row", "col", None),
        P("row", "col", None),
        P(),
        P(("row", "col"), None),
        P(("row", "col")),
        P(None, ("row", "col")),
        P(("row", "col")),
    )
    return jax.shard_map(
        local, mesh=mesh, in_specs=placed, out_specs=P(None, "row", "col", None), check_vma=False
    )
```

profile of v0, /device:TPU:0, one launch (start us, length us, event | category | flops | bytes accessed | tf_op | source)
XLA Modules:
  0.0 1200.3 jit_solution(8615943072689557903)
XLA Ops:
  13.8 18.0 %copy.299 = f32[6,8,16,512]{0,3,2,1:T(8,128)} copy(f32[6,8,16,512]{3,2,1,0:T(8,128)} %param.10) | data formatting | bytes 3145728 | tf_op args[0]
  31.7 13.4 %gather_fusion = f32[1024,6]{1,0:T(8,128)S(1)} fusion(f32[6,65536]{0,1:T(8,128)} %bitcast.155, s32[1024]{0:T(1024)S(1)} %get-tuple-element.56), kind=kCustom, calls=%fused_computation | custom fusion | bytes 53248 | tf_op jit(solution)/shard_map/gather | solution.py:49
  45.4 13.4 %gather_fusion.1 = f32[1024,6]{1,0:T(8,128)S(1)} fusion(f32[6,65536]{0,1:T(8,128)} %bitcast.156, s32[1024]{0:T(1024)S(1)} %get-tuple-element.58), kind=kCustom, calls=%fused_computation.1 | custom fusion | bytes 53248 | tf_op jit(solution)/shard_map/gather | solution.py:49
  59.7 13.3 %gather_fusion.2 = f32[1024,6]{1,0:T(8,128)S(1)} fusion(f32[6,65536]{0,1:T(8,128)} %bitcast.157, s32[1024]{0:T(1024)S(1)} %get-tuple-element.59), kind=kCustom, calls=%fused_computation.2 | custom fusion | bytes 53248 | tf_op jit(solution)/shard_map/gather | solution.py:49
  74.0 13.3 %gather_fusion.3 = f32[1024,6]{1,0:T(8,128)S(1)} fusion(f32[6,65536]{0,1:T(8,128)} %bitcast.158, s32[1024]{0:T(1024)S(1)} %get-tuple-element.57), kind=kCustom, calls=%fused_computation.3 | custom fusion | bytes 53248 | tf_op jit(solution)/shard_map/gather | solution.py:49
  88.3 13.3 %gather_fusion.4 = f32[1024,6]{1,0:T(8,128)S(1)} fusion(f32[6,65536]{0,1:T(8,128)} %bitcast.159, s32[1024]{0:T(1024)S(1)} %get-tuple-element.60), kind=kCustom, calls=%fused_computation.4 | custom fusion | bytes 53248 | tf_op jit(solution)/shard_map/gather | solution.py:49
  102.6 13.4 %gather_fusion.5 = f32[1024,6]{1,0:T(8,128)S(1)} fusion(f32[6,65536]{0,1:T(8,128)} %bitcast.160, s32[1024]{0:T(1024)S(1)} %get-tuple-element.63), kind=kCustom, calls=%fused_computation.5 | custom fusion | bytes 53248 | tf_op jit(solution)/shard_map/gather | solution.py:49
  117.0 13.3 %gather_fusion.6 = f32[1024,6]{1,0:T(8,128)S(1)} fusion(f32[6,65536]{0,1:T(8,128)} %bitcast.161, s32[1024]{0:T(1024)S(1)} %get-tuple-element.61), kind=kCustom, calls=%fused_computation.6 | custom fusion | bytes 53248 | tf_op jit(solution)/shard_map/gather | solution.py:49
  165.4 70.6 %custom-call.46 = f32[6,128,128]{2,1,0:T(8,128)S(1)} custom-call(f32[6,128,128]{2,1,0:T(8,128)S(1)} %cholesky.313), custom_call_target="Cholesky" | custom-call | tf_op jit(solution)/shard_map/vmap(jit(cholesky))/cholesky | solution.py:29
  236.0 59.0 %custom-call.47 = f32[6,1,128,128]{2,3,1,0:T(8,128)S(1)} custom-call(f32[6,1,128,128]{3,2,1,0:T(8,128)S(1)} %select_bitcast_fusion.2), custom_call_target="InvertDiagBlocksLowerTriangular" | custom-call | tf_op jit(solution)/shard_map/vmap(jit(cholesky))/cholesky | solution.py:29
  304.4 70.7 %custom-call.48 = f32[6,128,128]{2,1,0:T(8,128)S(1)} custom-call(f32[6,128,128]{2,1,0:T(8,128)S(1)} %cholesky.317), custom_call_target="Cholesky" | custom-call | tf_op jit(solution)/shard_map/vmap(jit(cholesky))/cholesky | solution.py:29
  376.0 58.9 %custom-call.49 = f32[6,1,128,128]{2,3,1,0:T(8,128)S(1)} custom-call(f32[6,1,128,128]{3,2,1,0:T(8,128)S(1)} %get-tuple-element.46), custom_call_target="InvertDiagBlocksLowerTriangular" | custom-call | tf_op jit(solution)/shard_map/vmap(jit(cholesky))/cholesky | solution.py:29
  440.2 70.5 %custom-call.50 = f32[6,128,128]{2,1,0:T(8,128)S(1)} custom-call(f32[6,128,128]{2,1,0:T(8,128)S(1)} %cholesky.322), custom_call_target="Cholesky" | custom-call | tf_op jit(solution)/shard_map/vmap(jit(cholesky))/cholesky | solution.py:29
  511.6 58.9 %custom-call.51 = f32[6,1,128,128]{2,3,1,0:T(8,128)S(1)} custom-call(f32[6,1,128,128]{3,2,1,0:T(8,128)S(1)} %get-tuple-element.44), custom_call_target="InvertDiagBlocksLowerTriangular" | custom-call | tf_op jit(solution)/shard_map/vmap(jit(cholesky))/cholesky | solution.py:29
  575.4 70.5 %custom-call.52 = f32[6,128,128]{2,1,0:T(8,128)S(1)} custom-call(f32[6,128,128]{2,1,0:T(8,128)S(1)} %convolution_subtract_fusion.2), custom_call_target="Cholesky" | custom-call | tf_op jit(solution)/shard_map/vmap(jit(cholesky))/cholesky | solution.py:29
  669.9 31.1 %scatter_custom_fusion = f32[6,65536]{0,1:T(8,128)} fusion(f32[6,65536]{0,1:T(8,128)} %bitcast.163, s32[1024]{0:T(1024)} %get-tuple-element.55, f32[6,1024]{0,1:T(8,128)S(1)} %bitcast.179, pred[1024]{0:T(1024)(128)(4,1)S(1)} %fusion.84, s32[1024]{0:T(1024)S(1)} %copy-done.18), kind=kCustom, calls=%fused_computation.83 | custom fusion | flops 6144 | bytes 35156992 | tf_op jit(solution)/shard_map/scatter | solution.py:73
  701.1 19.6 %copy.312 = f32[6,8,16,512]{3,2,1,0:T(8,128)S(1)} copy(f32[6,8,16,512]{0,3,2,1:T(8,128)} %bitcast.164) | data formatting | bytes 3145728 | tf_op jit(solution)/shard_map/reshape | solution.py:74
  725.1 15.3 %while.1 = (s32[]{:T(128)}, f32[6,512,512]{2,1,0:T(8,128)}, s32[4,2]{0,1:T(2,128)S(1)}, f32[4,6,128,128]{3,2,0,1:T(8,128)}, s32[]{:T(128)}) while((s32[]{:T(128)}, f32[6,512,512]{2,1,0:T(8,128)}, s32[4,2]{0,1:T(2,128)S(1)}, f32[4,6,128,128]{3,2,0,1:T(8,128)}, s32[]{:T(128)}) %tuple.54), condition=%wide.while_cond, body=%wide.while_body.sunk | while | flops 2 | bytes 788065 | solution.py:36
  740.4 237.2 %custom-call.53 = f32[6,4,128,128]{2,3,1,0:T(8,128)} custom-call(f32[6,4,128,128]{3,2,1,0:T(8,128)} %bitcast.191), custom_call_target="InvertDiagBlocksLowerTriangular" | custom-call | tf_op jit(solution)/shard_map/vmap(jit(_cho_solve))/triangular_solve | solution.py:36
  1017.6 35.2 %custom-call.55 = f32[6,64,64]{2,1,0:T(8,128)S(1)} custom-call(f32[6,64,64]{2,1,0:T(8,128)S(1)} %fusion.75), custom_call_target="Cholesky" | custom-call | tf_op jit(solution)/shard_map/vmap(jit(cholesky))/cholesky | solution.py:29
  1053.1 29.5 %custom-call.57 = f32[6,1,64,64]{2,3,1,0:T(8,128)S(1)} custom-call(f32[6,1,64,64]{3,2,1,0:T(8,128)S(1)} %select_bitcast_fusion.3), custom_call_target="InvertDiagBlocksLowerTriangular" | custom-call | tf_op jit(solution)/shard_map/vmap(jit(_cho_solve))/triangular_solve | solution.py:36
  1087.6 24.9 %all_to_all.87 = f32[6,64,2,512]{3,2,0,1:T(2,128)S(1)} all-to-all(f32[6,64,2,512]{3,2,0,1:T(2,128)S(1)} %copy.331), channel_id=1, replica_groups=mesh['row'=8,'col'=4] {'row'}, dimensions={1} | all-to-all | bytes 3145728 | tf_op jit(solution)/shard_map/all_to_all | solution.py:103
  1114.1 40.2 %all_to_all.88 = f32[6,8,16,512]{3,2,0,1:T(8,128)S(1)} all-to-all(f32[6,8,16,512]{3,2,0,1:T(8,128)S(1)} %copy.334), channel_id=1, replica_groups=mesh['row'=8,'col'=4] {'col'}, dimensions={1} | all-to-all | bytes 3145728 | tf_op jit(solution)/shard_map/all_to_all | solution.py:104
  1159.5 39.0 %all_to_all.89 = f32[6,2,64,512]{3,1,0,2:T(2,128)S(1)} all-to-all(f32[6,2,64,512]{3,1,0,2:T(2,128)S(1)} %bitcast.177), channel_id=1, replica_groups=mesh['row'=8,'col'=4] {'col'}, dimensions={2} | all-to-all | bytes 3145728 | tf_op jit(solution)/shard_map/all_to_all | solution.py:112
  (189 shorter events, 171.9 us)
Async XLA Ops:
  1.3 654.1 %all-to-all-start = ((s32[1,32,1]{2,0,1:T(1,128)}), s32[1,32,1]{2,0,1:T(1,128)}, u32[]{:S(2)}, u32[]{:S(2)}) async-start(s32[1,32,1]{2,0,1:T(1,128)} %copy.300), calls=%async_computation | async-start | bytes 32768 | tf_op jit(solution)/shard_map/all_to_all | solution.py:67
  13.8 18.0 %copy-start.21 = (s32[1024]{0:T(1024)S(1)}, s32[1024]{0:T(1024)}, u32[]{:S(2)}) copy-start(s32[1024]{0:T(1024)} %param.14) | copy-start | bytes 12292
  101.7 43.9 %copy-start.19 = (f32[3,1024]{1,0:T(4,128)S(1)}, f32[3,1024]{1,0:T(4,128)}, u32[]{:S(2)}) copy-start(f32[3,1024]{1,0:T(4,128)} %param.15) | copy-start | bytes 36868
  102.6 47.2 %copy-start.22 = (s32[1024]{0:T(1024)S(1)}, s32[1024]{0:T(1024)}, u32[]{:S(2)}) copy-start(s32[1024]{0:T(1024)} %param.16) | copy-start | bytes 12292
  570.6 75.4 %copy-start.17 = (pred[128,128]{1,0:T(8,128)(4,1)S(1)}, pred[128,128]{1,0:T(8,128)(4,1)}, u32[]{:S(2)}) copy-start(pred[128,128]{1,0:T(8,128)(4,1)} %iota_compare_fusion.5) | copy-start | bytes 49156
  647.2 7.2 copy-start.3
  647.2 7.2 copy-start.4
  647.2 7.2 copy-start.5
  647.3 7.2 copy-start.6
  647.3 7.2 copy-start.7
  647.3 7.2 copy-start.8
  647.3 7.2 copy-start.9
  647.3 7.2 copy-start.11
  647.3 7.2 copy-start.12
  654.5 15.4 %copy-start.18 = (s32[1024]{0:T(1024)S(1)}, s32[1024]{0:T(1024)}, u32[]{:S(2)}) copy-start(s32[1024]{0:T(1024)} %get-tuple-element.54) | copy-start | bytes 12292
  655.4 13.0 %all-to-all-start.1 = ((f32[32,1,192]{2,1,0:T(1,128)}), f32[32,1,192]{2,1,0:T(1,128)S(1)}, u32[]{:S(2)}, u32[]{:S(2)}) async-start(f32[32,1,192]{2,1,0:T(1,128)} %reshape.370), calls=%async_computation.1 | async-start | bytes 65536 | tf_op jit(solution)/shard_map/all_to_all | solution.py:66
  701.1 24.0 %copy-start.23 = (s32[4]{0:T(128)S(1)}, s32[4]{0:T(128)}, u32[]{:S(2)}) copy-start(s32[4]{0:T(128)} %iota_multiply_fusion) | copy-start | bytes 52
  720.7 256.9 %collective-permute-start = (f32[6,1,16,512]{3,2,1,0:T(8,128)S(1)}, f32[6,1,16,512]{3,2,1,0:T(8,128)S(1)}, u32[]{:S(2)}, u32[]{:S(2)}) collective-permute-start(f32[6,1,16,512]{3,2,1,0:T(8,128)S(1)} %get-tuple-element.42), channel_id=1, source_target_pairs={{4,0},{8,4},{12,8},{16,12},{20,16},{24,20},{28,24},{5,1},{9,5},{13... | collective-permute-start | bytes 589832 | tf_op jit(solution)/shard_map/ppermute | solution.py:15
  722.0 255.6 %collective-permute-start.1 = (f32[6,1,16,512]{3,2,1,0:T(8,128)S(1)}, f32[6,1,16,512]{3,2,1,0:T(8,128)S(1)}, u32[]{:S(2)}, u32[]{:S(2)}) collective-permute-start(f32[6,1,16,512]{3,2,1,0:T(8,128)S(1)} %get-tuple-element.41), channel_id=1, source_target_pairs={{0,4},{4,8},{8,12},{12,16},{16,20},{20,24},{24,28},{1,5},{5,9},{9,... | collective-permute-start | bytes 589832 | tf_op jit(solution)/shard_map/ppermute | solution.py:14
  977.8 8.0 collective-permute-start.2
  979.1 8.1 copy-start.10
  979.2 8.1 copy-start.20
  979.2 8.1 collective-permute-start.3
  1013.4 69.2 %all-to-all-start.2 = ((f32[6,8,16,512]{3,1,0,2:T(8,128)}), f32[6,8,16,512]{3,1,0,2:T(8,128)S(1)}, u32[]{:S(2)}, u32[]{:S(2)}) async-start(f32[6,8,16,512]{3,1,0,2:T(8,128)} %copy.328), calls=%async_computation.2 | async-start | bytes 3145728 | tf_op jit(solution)/shard_map/all_to_all | solution.py:100
  (7 other events, 36.0 us)
where the time goes:
time: 1210 us; the launch traced here: 1200 us
  other arithmetic  813 us (67%)
  local copies, waits for them, and re-layouts  200 us (17%)
  blocking collectives  104 us (9%)
  matrix products  46.4 us (4%)
  starting transfers between devices  27.1 us (2%)
    another operation x20, other arithmetic, implicit_factor(): jnp.linalg.cholesky(identity + one_rate * operator_matrix)  498 us
    another operation x7, other arithmetic, solve_lines(): jax.scipy.linalg.cho_solve((factor_one, True), right_side)  275 us
    gather x16, local copies, waits for them, and re-layouts, interpolate(): flat_block[:, base_index + shift_j * k_cells * l_cells + shift_k * l_cell...  114 us
    all_to_all x1, blocking collectives, local(): lax.all_to_all(along_j, 'col', split_axis=1, concat_axis=2, tiled=True)  40.2 us
    all_to_all x1, blocking collectives, local(): lax.all_to_all(solved_k, 'col', split_axis=2, concat_axis=1, tiled=True)  39 us
    scatter x1, other arithmetic, local(): flat_block.at[:, fringe_cell]  31.1 us
    another operation x18, matrix products, solve_lines(): jax.scipy.linalg.cho_solve((factor_one, True), right_side)  26.8 us
    all_to_all x1, blocking collectives, local(): lax.all_to_all(solved_j, 'row', split_axis=1, concat_axis=2, tiled=True)  24.9 us
  transfers between devices with their start and end apart: 7, of which 3 were waited for; matrix products, arithmetic and copies ran while one was open for 80% of the time, Pallas kernels for 0%

commit v1 on v0

v1 whole, which is shorter than its diff:
```python
import functools

import jax
import jax.numpy as jnp
import ml_dtypes
import numpy as np
from jax import lax
from jax.experimental import pallas as pl
from jax.experimental.pallas import tpu as pltpu
from jax.sharding import PartitionSpec as P

F32 = jnp.float32
BF16 = jnp.bfloat16
MESH = pl.DeviceIdType.MESH
CHUNK = 1024


def dot(a, b):
    return jnp.dot(a, b, precision=lax.Precision.HIGHEST, preferred_element_type=F32)


def split(a):
    high = a.astype(BF16)
    return high, (a - high.astype(F32)).astype(BF16)


def dot_split(a, b_high, b_low):
    a_high, a_low = split(a)
    single = functools.partial(jnp.dot, preferred_element_type=F32)
    return single(a_high, b_high) + single(a_low, b_high) + single(a_high, b_low)


def iota(shape, dim):
    return lax.broadcasted_iota(jnp.int32, shape, dim)


def decay(distance, theta):
    return jnp.exp(-distance * theta)


def line_matrices(par, v, scales, position, block, total, local_of, other_of, others):
    rows = block * others
    theta = (par[v, 0], par[v, 1])
    first = (position * block).astype(F32)
    n1 = float(total + 1)
    r, q = iota((rows, rows), 0), iota((rows, rows), 1)
    i = first + local_of(r).astype(F32) + 1.0
    j = first + local_of(q).astype(F32) + 1.0
    low, high = jnp.minimum(i, j), jnp.maximum(i, j)
    own = jnp.zeros((rows, rows), F32)
    for m in (0, 1):
        own = own + scales[m] * decay(high - low, theta[m]) * (1.0 - decay(2.0 * low, theta[m])) * (
            1.0 - decay(2.0 * (n1 - high), theta[m])
        )
    own = jnp.where(other_of(r) == other_of(q), own, 0.0)

    def side_mode_other(t):
        side = t >= 2 * others
        within = jnp.where(side, t - 2 * others, t)
        mode = within >= others
        return side, mode, jnp.where(mode, within - others, within)

    r, q = iota((4 * others, rows), 0), iota((4 * others, rows), 1)
    side, mode, other = side_mode_other(r)
    angle = jnp.where(mode, theta[1], theta[0])
    j = local_of(q).astype(F32) + 1.0
    distance = jnp.where(side, j, block + 1.0 - j)
    edge = jnp.where(side, n1 - first - j, first + j)
    outgoing = decay(distance, angle) * (1.0 - decay(2.0 * edge, angle))
    outgoing = jnp.where(other == other_of(q), outgoing, 0.0)

    r, q = iota((rows, 4 * others), 0), iota((rows, 4 * others), 1)
    side, mode, other = side_mode_other(q)
    angle = jnp.where(mode, theta[1], theta[0])
    i = local_of(r).astype(F32) + 1.0
    distance = jnp.where(side, block - i, i - 1.0)
    edge = jnp.where(side, first + i, n1 - first - i)
    incoming = decay(distance, angle) * (1.0 - decay(2.0 * edge, angle)) * jnp.where(mode, scales[1], scales[0])
    incoming = jnp.where(other == other_of(r), incoming, 0.0)
    return own, outgoing, incoming


def kernel(
    nrow, ncol, bj, bk,
    x_ref, spec_ref, par, base_ref, frac_ref, alive_ref, cell_ref, shape_ref, sh_ref, sl_ref,
    out_ref,
    sent_ref, arr_ref, val_ref, fill_ref, upd_ref, mask_ref,
    hj_lo, hj_hi, hk_lo, hk_hi, ks_lo, ks_hi,
    gj, wj, uj, gk, wk, uk,
    own_j, in_j, snd_j, own_k, in_k, snd_k,
    f_send, f_recv, h_send, h_recv, j_send, j_recv, k_send, k_recv,
):
    nv, rows, bl = x_ref.shape
    ndev = nrow * ncol
    r, c = lax.axis_index("row"), lax.axis_index("col")
    me = r * ncol + c
    slots = base_ref.shape[1]
    cap = slots // ndev
    shift_k = bk.bit_length() - 1
    shift_l = bl.bit_length() - 1

    barrier = pltpu.get_barrier_semaphore()

    @pl.loop(1, ndev)
    def _(d):
        p = lax.rem(me + d, ndev)
        pl.semaphore_signal(barrier, inc=1, device_id=(p // ncol, lax.rem(p, ncol)), device_id_type=MESH)

    for t0 in range(0, slots, CHUNK):
        lanes = pl.ds(t0, CHUNK)
        base = base_ref[:, lanes]
        fj, fk, fl = frac_ref[0:1, lanes], frac_ref[1:2, lanes], frac_ref[2:3, lanes]
        cell_row = lax.shift_right_logical(base, shift_l)
        cell_l = base & (bl - 1)
        row = iota((rows, CHUNK), 0)
        weight = jnp.zeros((rows, CHUNK), F32)
        for a in (0, 1):
            for b in (0, 1):
                w = (fj if a else 1.0 - fj) * (fk if b else 1.0 - fk)
                weight = weight + jnp.where(row == cell_row + (a * bk + b), w, 0.0)
        w_high, w_low = split(weight)
        lane = iota((bl, CHUNK), 0)
        weight_l = jnp.where(lane == cell_l, 1.0 - fl, 0.0) + jnp.where(lane == cell_l + 1, fl, 0.0)
        for v in range(nv):
            x_high, x_low = split(x_ref[v].T)
            single = functools.partial(jnp.dot, preferred_element_type=F32)
            part = single(x_high, w_high) + single(x_low, w_high) + single(x_high, w_low)
            val_ref[v : v + 1, lanes] = jnp.sum(part * weight_l, axis=0, keepdims=True)
        val_ref[nv : nv + 1, lanes] = alive_ref[:, lanes]
    for p in range(ndev):
        sent_ref[p, :, 0:cap] = val_ref[:, p * cap : (p + 1) * cap]

    pl.semaphore_wait(barrier, ndev - 1)

    def fringe(p, q):
        return pltpu.make_async_remote_copy(
            src_ref=sent_ref.at[p], dst_ref=arr_ref.at[q], send_sem=f_send.at[p], recv_sem=f_recv.at[q],
            device_id=(p // ncol, lax.rem(p, ncol)), device_id_type=MESH,
        )

    @pl.loop(1, ndev)
    def _(d):
        fringe(lax.rem(me + d, ndev), me).start()

    arr_ref[me] = sent_ref[me]

    @pl.loop(0, nv)
    def _(v):
        own, outgoing, incoming = line_matrices(
            par, v, (par[v, 2], par[v, 3]), r, bj, bj * nrow,
            lambda t: lax.shift_right_logical(t, shift_k), lambda t: t & (bk - 1), bk,
        )
        gj[v], wj[v], uj[v] = own, outgoing, incoming
        own, outgoing, incoming = line_matrices(
            par, v, (par[v, 4], par[v, 5]), c, bk, bk * ncol,
            lambda t: t & (bk - 1), lambda t: lax.shift_right_logical(t, shift_k), bj,
        )
        gk[v], wk[v], uk[v] = own, outgoing, incoming

    @pl.loop(1, ndev)
    def _(d):
        p = lax.rem(me + ndev - d, ndev)
        fringe(p, p).wait_recv()

    for p in range(ndev):
        val_ref[:, p * cap : (p + 1) * cap] = arr_ref[p, :, 0:cap]

    mask_ref[...] = jnp.zeros_like(mask_ref)
    fill_ref[...] = jnp.zeros_like(fill_ref)
    contract = (((1,), (1,)), ((), ()))
    for t0 in range(0, slots, CHUNK):
        lanes = pl.ds(t0, CHUNK)
        cell = cell_ref[:, lanes]
        alive = val_ref[nv : nv + 1, lanes] > 0.5
        at_row = (iota((rows, CHUNK), 0) == lax.shift_right_logical(cell, shift_l)) & alive
        at_lane = jnp.where(iota((bl, CHUNK), 0) == (cell & (bl - 1)), 1.0, 0.0).astype(BF16)
        place = functools.partial(lax.dot_general, dimension_numbers=contract, preferred_element_type=F32)
        mask_ref[...] += place(jnp.where(at_row, 1.0, 0.0).astype(BF16), at_lane)
        for v in range(nv):
            value = jnp.where(at_row, val_ref[v : v + 1, lanes], 0.0)
            high, low = split(value)
            rest = (value - high.astype(F32) - low.astype(F32)).astype(BF16)
            fill_ref[v] += place(high, at_lane) + place(low, at_lane) + place(rest, at_lane)

    @pl.loop(0, nv)
    def _(v):
        filled = jnp.where(mask_ref[...] > 0.5, fill_ref[v], x_ref[v])
        fill_ref[v] = filled
        planes = filled.reshape(bj, bk, bl)
        ks_lo[v] = planes[:, bk - 1, :]
        ks_hi[v] = planes[:, 0, :]

    halos = (
        (r < nrow - 1, r > 0, fill_ref.at[:, pl.ds(rows - bk, bk)], hj_lo, (r + 1, c)),
        (r > 0, r < nrow - 1, fill_ref.at[:, pl.ds(0, bk)], hj_hi, (r - 1, c)),
        (c < ncol - 1, c > 0, ks_lo, hk_lo, (r, c + 1)),
        (c > 0, c < ncol - 1, ks_hi, hk_hi, (r, c - 1)),
    )

    def halo(h):
        _, _, source, target, device = halos[h]
        return pltpu.make_async_remote_copy(
            src_ref=source, dst_ref=target, send_sem=h_send.at[h], recv_sem=h_recv.at[h],
            device_id=device, device_id_type=MESH,
        )

    for h in range(4):
        pl.when(halos[h][0])(lambda h=h: halo(h).start())

        @pl.when(jnp.logical_not(halos[h][1]))
        def _(h=h):
            halos[h][3][...] = jnp.zeros_like(halos[h][3])

    for h in range(4):
        pl.when(halos[h][1])(lambda h=h: halo(h).wait_recv())

    lane = iota((rows, bl), 1)
    k_of = iota((rows, bl), 0) & (bk - 1)

    def spread(plane):
        return jnp.broadcast_to(plane[:, None, :], (bj, bk, bl)).reshape(rows, bl)

    @pl.loop(0, nv)
    def _(v):
        f = fill_ref[v]
        total = jnp.concatenate([f[bk:], hj_hi[v]], axis=0) + jnp.concatenate([hj_lo[v], f[:-bk]], axis=0)
        total = total + jnp.where(k_of == bk - 1, spread(hk_hi[v]), pltpu.roll(f, rows - 1, 0))
        total = total + jnp.where(k_of == 0, spread(hk_lo[v]), pltpu.roll(f, 1, 0))
        total = total + jnp.where(lane == bl - 1, 0.0, pltpu.roll(f, bl - 1, 1))
        total = total + jnp.where(lane == 0, 0.0, pltpu.roll(f, 1, 1))
        u = par[v, 6] * (spec_ref[...] * (total - 6.0 * f))
        upd_ref[v] = u
        own_j[v] = dot(wj[v], u)

    def chain(position, count, place_of, half, own, arrive, send, s_sem, r_sem, alpha):
        def hop(side, v):
            target = place_of(position + (1 if side == 0 else -1))
            return pltpu.make_async_remote_copy(
                src_ref=send.at[side, v], dst_ref=arrive.at[v, pl.ds(side * half, half)],
                send_sem=s_sem.at[side, v], recv_sem=r_sem.at[side, v], device_id=target, device_id_type=MESH,
            )

        has_in = (position > 0, position < count - 1)
        has_out = (position < count - 1, position > 0)

        def pass_on(side):
            @pl.when(jnp.logical_not(has_in[side]))
            def _():
                arrive[:, pl.ds(side * half, half), :] = jnp.zeros((nv, half, bl), F32)

            @pl.loop(0, nv)
            def _(v):
                pl.when(has_in[side])(lambda: hop(side, v).wait_recv())

                @pl.when(has_out[side])
                def _():
                    came = arrive[v, pl.ds(side * half, half), :]
                    factor = jnp.where(iota((half, bl), 0) < half // 2, par[v, alpha], par[v, alpha + 1])
                    send[side, v] = own[v, pl.ds(side * half, half), :] + factor * came
                    hop(side, v).start()

        @pl.when(position < count // 2)
        def _():
            pass_on(0)
            pass_on(1)

        @pl.when(position >= count // 2)
        def _():
            pass_on(1)
            pass_on(0)

        def finish():
            for side in (0, 1):

                @pl.when(has_out[side])
                def _(side=side):
                    @pl.loop(0, nv)
                    def _(v):
                        hop(side, v).wait_send()

        return finish

    finish_j = chain(r, nrow, lambda p: (p, c), 2 * bk, own_j, in_j, snd_j, j_send, j_recv, 7)

    @pl.loop(0, nv)
    def _(v):
        y = dot(gj[v], upd_ref[v]) + dot(uj[v], in_j[v])
        upd_ref[v] = y
        own_k[v] = dot(wk[v], y)

    finish_k = chain(c, ncol, lambda p: (r, p), 2 * bj, own_k, in_k, snd_k, k_send, k_recv, 9)

    @pl.loop(0, nv)
    def _(v):
        y = dot(gk[v], upd_ref[v]) + dot(uk[v], in_k[v])
        wave = dot_split(y, sh_ref[...], sl_ref[...])
        wave = wave / (par[v, 11] + par[v, 6] * shape_ref[...])
        out_ref[v] = dot_split(wave, sh_ref[...], sl_ref[...])

    finish_j()
    finish_k()
    for h in range(4):
        pl.when(halos[h][0])(lambda h=h: halo(h).wait_send())

    @pl.loop(1, ndev)
    def _(d):
        fringe(lax.rem(me + d, ndev), me).wait_send()


def parameters(step, bj, bk, nrow, ncol):
    product = 3.5 * step
    diagonal = 1.0 + product
    unit = (diagonal - product) - ((4.0 * step - product) - 0.5 * step)
    unit = unit / 1.0
    s = step / unit
    root = jnp.sqrt(1.0 - 1.0 / s)
    b = 2.0 + 2.0 * root
    a = 4.0 / (s * b)
    kappa = 1.0 / (s * root * unit)

    def angle(x):
        return 2.0 * jnp.arcsinh(0.5 * jnp.sqrt(x))

    def scale(x, theta, n):
        return kappa / (2.0 * jnp.sqrt(x + 0.25 * x * x) * (1.0 - jnp.exp(-2.0 * (n + 1) * theta)))

    ta, tb = angle(a), angle(b)
    nj, nk = bj * nrow, bk * ncol
    return jnp.stack(
        [
            ta, tb, scale(a, ta, nj), -scale(b, tb, nj), scale(a, ta, nk), -scale(b, tb, nk), step,
            jnp.exp(-bj * ta), jnp.exp(-bj * tb), jnp.exp(-bk * ta), jnp.exp(-bk * tb), unit,
        ],
        axis=1,
    )


def sine_constants(n):
    k = np.arange(1, n + 1)
    s = np.sqrt(2.0 / (n + 1)) * np.sin(np.pi * ((k[:, None] * k[None, :]) % (2 * (n + 1))) / (n + 1))
    high = s.astype(ml_dtypes.bfloat16)
    low = (s - high.astype(np.float64)).astype(ml_dtypes.bfloat16)
    lam = 4.0 * np.sin(np.pi * k / (2.0 * (n + 1))) ** 2
    return high, low, (lam + 0.25 * lam * lam).astype(np.float32)[None, :]


def local(nrow, ncol, flow_state, spectral, step_size, fringe_count, donor_base, donor_frac, fringe_cell):
    nv, bj, bk, bl = flow_state.shape
    rows = bj * bk
    ndev = nrow * ncol
    slots = donor_base.shape[0]
    cap = slots // ndev
    alive = (jnp.arange(cap, dtype=jnp.int32)[None, :] < fringe_count.reshape(ndev, 1)).astype(F32)
    high, low, shape = sine_constants(bl)
    vmem = pl.BlockSpec(memory_space=pltpu.VMEM)
    smem = pl.BlockSpec(memory_space=pltpu.SMEM)
    big = pltpu.VMEM((nv, rows, bl), F32)
    dma = pltpu.SemaphoreType.DMA
    out = pl.pallas_call(
        functools.partial(kernel, nrow, ncol, bj, bk),
        out_shape=jax.ShapeDtypeStruct((nv, rows, bl), F32),
        in_specs=[vmem, vmem, smem] + [vmem] * 7,
        out_specs=vmem,
        scratch_shapes=[
            pltpu.VMEM((ndev, 8, 128), F32),
            pltpu.VMEM((ndev, 8, 128), F32),
            pltpu.VMEM((8, slots), F32),
            big,
            big,
            pltpu.VMEM((rows, bl), F32),
            pltpu.VMEM((nv, bk, bl), F32),
            pltpu.VMEM((nv, bk, bl), F32),
            pltpu.VMEM((nv, bj, bl), F32),
            pltpu.VMEM((nv, bj, bl), F32),
            pltpu.VMEM((nv, bj, bl), F32),
            pltpu.VMEM((nv, bj, bl), F32),
            pltpu.VMEM((nv, rows, rows), F32),
            pltpu.VMEM((nv, 4 * bk, rows), F32),
            pltpu.VMEM((nv, rows, 4 * bk), F32),
            pltpu.VMEM((nv, rows, rows), F32),
            pltpu.VMEM((nv, 4 * bj, rows), F32),
            pltpu.VMEM((nv, rows, 4 * bj), F32),
            pltpu.VMEM((nv, 4 * bk, bl), F32),
            pltpu.VMEM((nv, 4 * bk, bl), F32),
            pltpu.VMEM((2, nv, 2 * bk, bl), F32),
            pltpu.VMEM((nv, 4 * bj, bl), F32),
            pltpu.VMEM((nv, 4 * bj, bl), F32),
            pltpu.VMEM((2, nv, 2 * bj, bl), F32),
            dma((ndev,)),
            dma((ndev,)),
            dma((4,)),
            dma((4,)),
            dma((2, nv)),
            dma((2, nv)),
            dma((2, nv)),
            dma((2, nv)),
        ],
        compiler_params=pltpu.CompilerParams(
            collective_id=0, has_side_effects=True, vmem_limit_bytes=56 * 1024 * 1024
        ),
    )(
        flow_state.reshape(nv, rows, bl),
        spectral.reshape(rows, bl),
        parameters(step_size, bj, bk, nrow, ncol),
        donor_base.reshape(1, slots),
        donor_frac,
        alive.reshape(1, slots),
        fringe_cell.reshape(1, slots),
        jnp.asarray(shape),
        jnp.asarray(high),
        jnp.asarray(low),
    )
    return out.reshape(nv, bj, bk, bl)


def solution(mesh):
    placed = (
        P(None, "row", "col", None),
        P("row", "col", None),
        P(),
        P(("row", "col"), None),
        P(("row", "col")),
        P(None, ("row", "col")),
        P(("row", "col")),
    )
    return jax.shard_map(
        functools.partial(local, mesh.shape["row"], mesh.shape["col"]),
        mesh=mesh, in_specs=placed, out_specs=P(None, "row", "col", None), check_vma=False,
    )
```

time: 1210 us -> 81.6 us (0.07)
  other arithmetic: 813 us -> 2.16 us
  local copies, waits for them, and re-layouts: 200 us -> 5.69 us
  blocking collectives: 104 us -> 0 us
  Pallas kernels: 0 us -> 73.5 us
  matrix products: 46.4 us -> 0 us
  starting transfers between devices: 27.1 us -> 0 us
    another operation x27 -> x3, other arithmetic: 773 us -> 1.44 us  [parameters(): jnp.stack([ta, tb, scale(a, ta, nj), -scale(b, tb, nj), scale(a, ta, nk),...]
    gather x16 -> x0, local copies, waits for them, and re-layouts: 114 us -> none  [interpolate(): flat_block[:, base_index + shift_j * k_cells * l_cells + shift_k * l_cell...]
    all_to_all x3 -> x0, blocking collectives: 104 us -> none  [the longest x1 40.2 us: local(): lax.all_to_all(along_j, 'col', split_axis=1, concat_axis=2, tiled=True)]
    pallas_call x0 -> x1, Pallas kernels: none -> 73.5 us  [local(): pl.pallas_call(functools.partial(kernel, nrow, ncol, bj, bk), out_shape=j...]
    another operation x24 -> x0, matrix products: 42.8 us -> none  [the longest x18 26.8 us: solve_lines(): jax.scipy.linalg.cho_solve((factor_one, True), right_side)]
    scatter x1 -> x0, other arithmetic: 31.1 us -> none  [local(): flat_block.at[:, fringe_cell]]
    reshape x9 -> x0, local copies, waits for them, and re-layouts: 26.1 us -> none  [the longest x1 19.6 us: local(): filled = flat_block.reshape(variables, block_j, block_k, block_l)]
    unnamed x51 -> x1, local copies, waits for them, and re-layouts: 21.5 us -> 2.77 us
  transfers between devices with their start and end apart: 7 -> 0, of which waited for: 3 -> 0; matrix products, arithmetic and copies ran while one was open for 80% -> 0% of each run, Pallas kernels for 0% -> 0%
where the time goes in v1:
time: 81.6 us; the launch traced here: 81.4 us
  Pallas kernels  73.5 us (90%)
  local copies, waits for them, and re-layouts  5.69 us (7%)
  other arithmetic  2.16 us (3%)
    pallas_call x1, Pallas kernels, local(): pl.pallas_call(functools.partial(kernel, nrow, ncol, bj, bk), out_shape=j...  73.5 us
    unnamed x1, local copies, waits for them, and re-layouts  2.77 us
    another operation x11, local copies, waits for them, and re-layouts, parameters(): jnp.stack([ta, tb, scale(a, ta, nj), -scale(b, tb, nj), scale(a, ta, nk),...  2.25 us

profile of v1, /device:TPU:0, one launch (start us, length us, event | category | flops | bytes accessed | tf_op | source)
XLA Modules:
  0.0 81.4 jit_solution(7571622463611003572)
XLA Ops:
  0.0 0.7 exponential_bitcast_fusion
  0.7 0.7 exponential_bitcast_fusion.1
  1.5 0.1 copy.14
  1.6 0.1 copy.20
  1.6 0.1 copy.21
  1.7 0.1 copy.13
  1.8 0.1 copy.18
  1.9 0.1 copy.11
  2.0 0.1 copy.19
  2.1 0.1 copy.12
  2.2 0.1 copy.22
  2.3 0.7 copy.17
  3.0 0.7 stack.45.par
  3.7 0.7 fusion
  4.4 0.7 reshape.50.alive_ref
  5.1 73.5 %shard_map.100 = f32[6,128,512]{2,1,0:T(8,128)} custom-call(f32[6,128,512]{2,1,0:T(8,128)} %bitcast.25, f32[128,512]{1,0:T(8,128)} %bitcast.26, f32[6,12]{1,0:T(8,128)} %stack.45.par, s32[1,1024]{1,0:T(1,128)} %bitcast.29, f32[3,1024]{1,0:T(4,128)} %frac_ref.1, f32[1,1024]{1,0:T(1,128)} %reshape.50.alive_ref, s32[1,1024]{1,0:T(1,128)} %bitcast.30, ...), custom_call_target="tpu_custom_call" | custom-call | tf_op jit(solution)/shard_map/pallas_call | solution.py:359
  78.6 2.8 %copy.24 = f32[6,8,16,512]{3,2,1,0:T(8,128)} copy(f32[6,8,16,512]{3,2,1,0:T(8,128)} %bitcast.24) | data formatting | bytes 3145728
  (1 shorter events, 0.0 us)

commit v2 on v1

v2 whole, which is shorter than its diff:
```python
import functools

import jax
import jax.numpy as jnp
import ml_dtypes
import numpy as np
from jax import lax
from jax.experimental import pallas as pl
from jax.experimental.pallas import tpu as pltpu
from jax.sharding import PartitionSpec as P

F32 = jnp.float32
BF16 = jnp.bfloat16
MESH = pl.DeviceIdType.MESH
CHUNK = 256


def split(a):
    high = a.astype(BF16)
    return high, (a - high.astype(F32)).astype(BF16)


def dot_split(a, b_high, b_low):
    a_high, a_low = split(a)
    single = functools.partial(jnp.dot, preferred_element_type=F32)
    return single(a_high, b_high) + single(a_low, b_high) + single(a_high, b_low)


def iota(shape, dim):
    return lax.broadcasted_iota(jnp.int32, shape, dim)


def decay(distance, theta):
    return jnp.exp(-distance * theta)


def dot3(a, b):
    b_high, b_low = split(b)
    return dot_split(a, b_high, b_low)


def line_matrices(theta, scales, position, block, total, local_of, other_of, others, expand):
    rows = block * others
    first = (position * block).astype(F32)
    n1 = float(total + 1)
    i = first + iota((block, rows), 0).astype(F32) + 1.0
    j = first + local_of(iota((block, rows), 1)).astype(F32) + 1.0
    low, high = jnp.minimum(i, j), jnp.maximum(i, j)
    own = jnp.zeros((block, rows), F32)
    for m in (0, 1):
        own = own + scales[m] * decay(high - low, theta[m]) * (1.0 - decay(2.0 * low, theta[m])) * (
            1.0 - decay(2.0 * (n1 - high), theta[m])
        )
    own = jnp.where(other_of(iota((rows, rows), 0)) == other_of(iota((rows, rows), 1)), expand(own), 0.0)

    j = local_of(iota((1, rows), 1)).astype(F32) + 1.0
    parts = []
    for side in (0, 1):
        for m in (0, 1):
            distance = j if side else block + 1.0 - j
            edge = n1 - first - j if side else first + j
            value = decay(distance, theta[m]) * (1.0 - decay(2.0 * edge, theta[m]))
            same = iota((others, rows), 0) == other_of(iota((others, rows), 1))
            parts.append(jnp.where(same, value, 0.0))
    outgoing = jnp.concatenate(parts, axis=0)

    width = 4 * others
    t = iota((block, width), 1)
    side = t >= 2 * others
    mode = jnp.where(side, t - 2 * others, t) >= others
    angle = jnp.where(mode, theta[1][:, :width], theta[0][:, :width])
    i = iota((block, width), 0).astype(F32) + 1.0
    distance = jnp.where(side, block - i, i - 1.0)
    edge = jnp.where(side, first + i, n1 - first - i)
    incoming = decay(distance, angle) * (1.0 - decay(2.0 * edge, angle))
    incoming = incoming * jnp.where(mode, scales[1][:, :width], scales[0][:, :width])
    other = iota((rows, width), 1) & (others - 1)
    incoming = jnp.where(other == other_of(iota((rows, width), 0)), expand(incoming), 0.0)
    return own, outgoing, incoming


def kernel(
    nrow, ncol, bj, bk,
    x_ref, spec_ref, step_ref, count_ref, base_ref, frac_ref, cell_ref, shape_ref, sh_ref, sl_ref,
    out_ref,
    sent_ref, arr_ref, val_ref, fill_ref, upd_ref, xh_ref, xl_ref, el_ref, lhs_ref, par_ref, inv_ref,
    hj_lo, hj_hi, hk_lo, hk_hi, ks_lo, ks_hi,
    gj, wj, uj, gk, wk, uk,
    own_j, in_j, snd_j, own_k, in_k, snd_k,
    f_send, f_recv, h_send, h_recv, j_send, j_recv, k_send, k_recv,
):
    nv, rows, bl = x_ref.shape
    ndev = nrow * ncol
    r, c = lax.axis_index("row"), lax.axis_index("col")
    me = r * ncol + c
    slots = base_ref.shape[1]
    cap = slots // ndev
    shift_k = bk.bit_length() - 1
    shift_l = bl.bit_length() - 1
    half_v = nv // 2
    single = functools.partial(jnp.dot, preferred_element_type=F32)

    barrier = pltpu.get_barrier_semaphore()

    @pl.loop(1, ndev)
    def _(d):
        p = lax.rem(me + d, ndev)
        pl.semaphore_signal(barrier, inc=1, device_id=(p // ncol, lax.rem(p, ncol)), device_id_type=MESH)

    @pl.loop(0, nv)
    def _(v):
        here = pl.ds(pl.multiple_of(v * rows, rows), rows)
        xh_ref[here, :], xl_ref[here, :] = split(x_ref[v])

    @pl.loop(0, slots // CHUNK)
    def _(t):
        lanes = pl.ds(pl.multiple_of(t * CHUNK, CHUNK), CHUNK)
        base = base_ref[:, lanes]
        fj, fk, fl = frac_ref[0:1, lanes], frac_ref[1:2, lanes], frac_ref[2:3, lanes]
        cell_row = lax.shift_right_logical(base, shift_l)
        cell_l = base & (bl - 1)
        row = iota((rows, CHUNK), 0)
        weight = jnp.zeros((rows, CHUNK), F32)
        for a in (0, 1):
            for b in (0, 1):
                w = (fj if a else 1.0 - fj) * (fk if b else 1.0 - fk)
                weight = jnp.where(row == cell_row + (a * bk + b), w, weight)
        lane = iota((bl, CHUNK), 0)
        weight_l = jnp.where(lane == cell_l, 1.0 - fl, jnp.where(lane == cell_l + 1, fl, 0.0))
        w_high, w_low = split(weight_l)
        part = single(xh_ref[...], w_high) + single(xl_ref[...], w_high) + single(xh_ref[...], w_low)
        part = part.reshape(nv, rows, CHUNK) * weight[None]
        val_ref[0:nv, lanes] = jnp.sum(part, axis=1)

    lane_cap = iota((1, cap), 1)
    for p in range(ndev):
        sent_ref[p, 0:nv, 0:cap] = val_ref[0:nv, p * cap : (p + 1) * cap]
        sent_ref[p, nv : nv + 1, 0:cap] = jnp.where(lane_cap < count_ref[0, p], 1.0, 0.0)

    pl.semaphore_wait(barrier, ndev - 1)

    def fringe(p, q):
        return pltpu.make_async_remote_copy(
            src_ref=sent_ref.at[p], dst_ref=arr_ref.at[q], send_sem=f_send.at[p], recv_sem=f_recv.at[q],
            device_id=(p // ncol, lax.rem(p, ncol)), device_id_type=MESH,
        )

    @pl.loop(1, ndev)
    def _(d):
        fringe(lax.rem(me + d, ndev), me).start()

    arr_ref[me] = sent_ref[me]

    @pl.loop(0, nv)
    def _(v):
        parameters(par_ref, v, step_ref[v], bj, bk, nrow, ncol)
        row = [par_ref[v, n : n + 1, :] for n in range(6)]
        gj[v], wj[v], uj[v] = line_matrices(
            row[0:2], row[2:4], r, bj, bj * nrow,
            lambda t: lax.shift_right_logical(t, shift_k), lambda t: t & (bk - 1), bk,
            lambda z: jnp.broadcast_to(z[:, None, :], (bj, bk, z.shape[1])).reshape(rows, z.shape[1]),
        )
        gk[v], wk[v], uk[v] = line_matrices(
            row[0:2], row[4:6], c, bk, bk * ncol,
            lambda t: t & (bk - 1), lambda t: lax.shift_right_logical(t, shift_k), bj,
            lambda z: jnp.broadcast_to(z[None], (bj, bk, z.shape[1])).reshape(rows, z.shape[1]),
        )
        inv_ref[v] = 1.0 / (par_ref[v, 11:12, 0:1] + step_ref[v] * shape_ref[...])

    @pl.loop(0, slots // CHUNK)
    def _(t):
        start = pl.multiple_of(t * CHUNK, CHUNK)
        cell = cell_ref[:, pl.ds(start, CHUNK)]
        at_lane = jnp.where(iota((bl, CHUNK), 0) == (cell & (bl - 1)), 1.0, 0.0)
        el_ref[pl.ds(start, CHUNK), :] = at_lane.T.astype(BF16)

    @pl.loop(1, ndev)
    def _(d):
        p = lax.rem(me + ndev - d, ndev)
        fringe(p, p).wait_recv()

    for p in range(ndev):
        val_ref[:, p * cap : (p + 1) * cap] = arr_ref[p, :, 0:cap]

    def halos(g):
        vs = pl.ds(g * half_v, half_v)
        return (
            (r < nrow - 1, r > 0, fill_ref.at[vs, pl.ds(rows - bk, bk)], hj_lo.at[vs], (r + 1, c)),
            (r > 0, r < nrow - 1, fill_ref.at[vs, pl.ds(0, bk)], hj_hi.at[vs], (r - 1, c)),
            (c < ncol - 1, c > 0, ks_lo.at[vs], hk_lo.at[vs], (r, c + 1)),
            (c > 0, c < ncol - 1, ks_hi.at[vs], hk_hi.at[vs], (r, c - 1)),
        )

    def halo(g, h):
        _, _, source, target, device = halos(g)[h]
        return pltpu.make_async_remote_copy(
            src_ref=source, dst_ref=target, send_sem=h_send.at[g, h], recv_sem=h_recv.at[g, h],
            device_id=device, device_id_type=MESH,
        )

    at_row = (iota((rows, slots), 0) == lax.shift_right_logical(cell_ref[...], shift_l)) & (
        val_ref[nv : nv + 1, :] > 0.5
    )
    mask = single(jnp.where(at_row, 1.0, 0.0).astype(BF16), el_ref[...]) > 0.5
    for g in (0, 1):
        for n in range(half_v):
            v = g * half_v + n
            high, low = split(jnp.where(at_row, val_ref[v : v + 1, :], 0.0))
            lhs_ref[2 * n * rows : (2 * n + 1) * rows, :] = high
            lhs_ref[(2 * n + 1) * rows : (2 * n + 2) * rows, :] = low
        placed = single(lhs_ref[...], el_ref[...])
        for n in range(half_v):
            v = g * half_v + n
            value = placed[2 * n * rows : (2 * n + 1) * rows] + placed[(2 * n + 1) * rows : (2 * n + 2) * rows]
            filled = jnp.where(mask, value, x_ref[v])
            fill_ref[v] = filled
            planes = filled.reshape(bj, bk, bl)
            ks_lo[v] = planes[:, bk - 1, :]
            ks_hi[v] = planes[:, 0, :]
        for h in range(4):
            pl.when(halos(g)[h][0])(lambda g=g, h=h: halo(g, h).start())

    for h, buffer in enumerate((hj_lo, hj_hi, hk_lo, hk_hi)):

        @pl.when(jnp.logical_not(halos(0)[h][1]))
        def _(buffer=buffer):
            buffer[...] = jnp.zeros_like(buffer)

    lane = iota((rows, bl), 1)
    k_of = iota((rows, bl), 0) & (bk - 1)

    def spread(plane):
        return jnp.broadcast_to(plane[:, None, :], (bj, bk, bl)).reshape(rows, bl)

    for g in (0, 1):
        for h in range(4):
            pl.when(halos(g)[h][1])(lambda g=g, h=h: halo(g, h).wait_recv())

        @pl.loop(g * half_v, (g + 1) * half_v)
        def _(v):
            f = fill_ref[v]
            total = jnp.concatenate([f[bk:], hj_hi[v]], axis=0) + jnp.concatenate([hj_lo[v], f[:-bk]], axis=0)
            total = total + jnp.where(k_of == bk - 1, spread(hk_hi[v]), pltpu.roll(f, rows - 1, 0))
            total = total + jnp.where(k_of == 0, spread(hk_lo[v]), pltpu.roll(f, 1, 0))
            total = total + jnp.where(lane == bl - 1, 0.0, pltpu.roll(f, bl - 1, 1))
            total = total + jnp.where(lane == 0, 0.0, pltpu.roll(f, 1, 1))
            u = step_ref[v] * (spec_ref[...] * (total - 6.0 * f))
            upd_ref[v] = u
            own_j[v] = dot3(wj[v], u)

    def solve_l(ref):
        count = ref.shape[1]
        for g in (0, 1):
            vs = pl.ds(g * half_v, half_v)
            wave = dot_split(ref[vs].reshape(half_v * count, bl), sh_ref[...], sl_ref[...])
            wave = (wave.reshape(half_v, count, bl) * inv_ref[vs]).reshape(half_v * count, bl)
            ref[vs] = dot_split(wave, sh_ref[...], sl_ref[...]).reshape(half_v, count, bl)

    def chain(position, count, place_of, half, own, arrive, send, s_sem, r_sem, alpha, meanwhile):
        def hop(side, v):
            target = place_of(position + (1 if side == 0 else -1))
            return pltpu.make_async_remote_copy(
                src_ref=send.at[side, v], dst_ref=arrive.at[v, pl.ds(side * half, half)],
                send_sem=s_sem.at[side, v], recv_sem=r_sem.at[side, v], device_id=target, device_id_type=MESH,
            )

        has_in = (position > 0, position < count - 1)
        has_out = (position < count - 1, position > 0)

        def pass_on(side):
            @pl.when(jnp.logical_not(has_in[side]))
            def _():
                arrive[:, pl.ds(side * half, half), :] = jnp.zeros((nv, half, bl), F32)

            @pl.loop(0, nv)
            def _(v):
                pl.when(has_in[side])(lambda: hop(side, v).wait_recv())

                @pl.when(has_out[side])
                def _():
                    came = arrive[v, pl.ds(side * half, half), :]
                    factor = jnp.where(
                        iota((half, bl), 0) < half // 2, par_ref[v, alpha : alpha + 1, 0:1], par_ref[v, alpha + 1 : alpha + 2, 0:1]
                    )
                    send[side, v] = own[v, pl.ds(side * half, half), :] + factor * came
                    hop(side, v).start()

        lower = position < count // 2
        upper = jnp.logical_not(lower)
        inner = (position >= count // 4) & (position < count - count // 4)
        pl.when(inner)(meanwhile)
        pl.when(lower)(lambda: pass_on(0))
        pl.when(upper)(lambda: pass_on(1))
        pl.when(jnp.logical_not(inner))(meanwhile)
        pl.when(lower)(lambda: pass_on(1))
        pl.when(upper)(lambda: pass_on(0))

        def finish():
            for side in (0, 1):

                @pl.when(has_out[side])
                def _(side=side):
                    @pl.loop(0, nv)
                    def _(v):
                        hop(side, v).wait_send()

        return finish

    def local_j():
        solve_l(upd_ref)

        @pl.loop(0, nv)
        def _(v):
            upd_ref[v] = dot3(gj[v], upd_ref[v])

    finish_j = chain(r, nrow, lambda p: (p, c), 2 * bk, own_j, in_j, snd_j, j_send, j_recv, 7, local_j)

    for g in (0, 1):
        vs = pl.ds(g * half_v, half_v)
        wave = dot_split(in_j[vs].reshape(half_v * 4 * bk, bl), sh_ref[...], sl_ref[...])
        wave = (wave.reshape(half_v, 4 * bk, bl) * inv_ref[vs]).reshape(half_v * 4 * bk, bl)
        own_j[vs] = dot_split(wave, sh_ref[...], sl_ref[...]).reshape(half_v, 4 * bk, bl)

    @pl.loop(0, nv)
    def _(v):
        y = upd_ref[v] + dot3(uj[v], own_j[v])
        upd_ref[v] = y
        own_k[v] = dot3(wk[v], y)

    def local_k():
        @pl.loop(0, nv)
        def _(v):
            out_ref[v] = dot3(gk[v], upd_ref[v])

    finish_k = chain(c, ncol, lambda p: (r, p), 2 * bj, own_k, in_k, snd_k, k_send, k_recv, 9, local_k)

    @pl.loop(0, nv)
    def _(v):
        out_ref[v] = out_ref[v] + dot3(uk[v], in_k[v])

    finish_j()
    finish_k()
    for g in (0, 1):
        for h in range(4):
            pl.when(halos(g)[h][0])(lambda g=g, h=h: halo(g, h).wait_send())

    @pl.loop(1, ndev)
    def _(d):
        fringe(lax.rem(me + d, ndev), me).wait_send()


def parameters(par_ref, v, step_scalar, bj, bk, nrow, ncol):
    step = jnp.full((1, 128), step_scalar, F32)
    product = 3.5 * step
    diagonal = 1.0 + product
    unit = (diagonal - product) - ((4.0 * step - product) - 0.5 * step)
    s = step / unit
    root = jnp.sqrt(1.0 - 1.0 / s)
    b = 2.0 + 2.0 * root
    a = 4.0 / (s * b)
    kappa = 1.0 / (s * root * unit)

    def angle(x):
        h = 0.5 * jnp.sqrt(x)
        return 2.0 * jnp.log1p(h + h * h / (1.0 + jnp.sqrt(1.0 + h * h)))

    def scale(x, theta, n):
        return kappa / (2.0 * jnp.sqrt(x + 0.25 * x * x) * (1.0 - jnp.exp(-2.0 * (n + 1) * theta)))

    ta, tb = angle(a), angle(b)
    nj, nk = bj * nrow, bk * ncol
    values = [
        ta, tb, scale(a, ta, nj), -scale(b, tb, nj), scale(a, ta, nk), -scale(b, tb, nk), step,
        jnp.exp(-bj * ta), jnp.exp(-bj * tb), jnp.exp(-bk * ta), jnp.exp(-bk * tb), unit,
    ]
    for n, value in enumerate(values):
        par_ref[v, n : n + 1, :] = value


def sine_constants(n):
    k = np.arange(1, n + 1)
    s = np.sqrt(2.0 / (n + 1)) * np.sin(np.pi * ((k[:, None] * k[None, :]) % (2 * (n + 1))) / (n + 1))
    high = s.astype(ml_dtypes.bfloat16)
    low = (s - high.astype(np.float64)).astype(ml_dtypes.bfloat16)
    lam = 4.0 * np.sin(np.pi * k / (2.0 * (n + 1))) ** 2
    return high, low, (lam + 0.25 * lam * lam).astype(np.float32)[None, :]


def local(nrow, ncol, flow_state, spectral, step_size, fringe_count, donor_base, donor_frac, fringe_cell):
    nv, bj, bk, bl = flow_state.shape
    rows = bj * bk
    ndev = nrow * ncol
    slots = donor_base.shape[0]
    high, low, shape = sine_constants(bl)
    vmem = pl.BlockSpec(memory_space=pltpu.VMEM)
    smem = pl.BlockSpec(memory_space=pltpu.SMEM)
    big = pltpu.VMEM((nv, rows, bl), F32)
    dma = pltpu.SemaphoreType.DMA
    out = pl.pallas_call(
        functools.partial(kernel, nrow, ncol, bj, bk),
        out_shape=jax.ShapeDtypeStruct((nv, rows, bl), F32),
        in_specs=[vmem, vmem, smem, smem] + [vmem] * 6,
        out_specs=vmem,
        scratch_shapes=[
            pltpu.VMEM((ndev, 8, 128), F32),
            pltpu.VMEM((ndev, 8, 128), F32),
            pltpu.VMEM((8, slots), F32),
            big,
            big,
            pltpu.VMEM((nv * rows, bl), BF16),
            pltpu.VMEM((nv * rows, bl), BF16),
            pltpu.VMEM((slots, bl), BF16),
            pltpu.VMEM((nv * rows, slots), BF16),
            pltpu.VMEM((nv, 16, 128), F32),
            pltpu.VMEM((nv, 1, bl), F32),
            pltpu.VMEM((nv, bk, bl), F32),
            pltpu.VMEM((nv, bk, bl), F32),
            pltpu.VMEM((nv, bj, bl), F32),
            pltpu.VMEM((nv, bj, bl), F32),
            pltpu.VMEM((nv, bj, bl), F32),
            pltpu.VMEM((nv, bj, bl), F32),
            pltpu.VMEM((nv, rows, rows), F32),
            pltpu.VMEM((nv, 4 * bk, rows), F32),
            pltpu.VMEM((nv, rows, 4 * bk), F32),
            pltpu.VMEM((nv, rows, rows), F32),
            pltpu.VMEM((nv, 4 * bj, rows), F32),
            pltpu.VMEM((nv, rows, 4 * bj), F32),
            pltpu.VMEM((nv, 4 * bk, bl), F32),
            pltpu.VMEM((nv, 4 * bk, bl), F32),
            pltpu.VMEM((2, nv, 2 * bk, bl), F32),
            pltpu.VMEM((nv, 4 * bj, bl), F32),
            pltpu.VMEM((nv, 4 * bj, bl), F32),
            pltpu.VMEM((2, nv, 2 * bj, bl), F32),
            dma((ndev,)),
            dma((ndev,)),
            dma((2, 4)),
            dma((2, 4)),
            dma((2, nv)),
            dma((2, nv)),
            dma((2, nv)),
            dma((2, nv)),
        ],
        compiler_params=pltpu.CompilerParams(
            collective_id=0, has_side_effects=True, vmem_limit_bytes=56 * 1024 * 1024
        ),
    )(
        flow_state.reshape(nv, rows, bl),
        spectral.reshape(rows, bl),
        step_size,
        fringe_count,
        donor_base.reshape(1, slots),
        donor_frac,
        fringe_cell.reshape(1, slots),
        jnp.asarray(shape),
        jnp.asarray(high),
        jnp.asarray(low),
    )
    return out.reshape(nv, bj, bk, bl)


def solution(mesh):
    placed = (
        P(None, "row", "col", None),
        P("row", "col", None),
        P(),
        P(("row", "col"), None),
        P(("row", "col")),
        P(None, ("row", "col")),
        P(("row", "col")),
    )
    return jax.shard_map(
        functools.partial(local, mesh.shape["row"], mesh.shape["col"]),
        mesh=mesh, in_specs=placed, out_specs=P(None, "row", "col", None), check_vma=False,
    )
```

time: 81.6 us -> 62.2 us (0.76)
  Pallas kernels: 73.5 us -> 59.3 us
  local copies, waits for them, and re-layouts: 5.69 us -> 2.77 us
  other arithmetic: 2.16 us -> 0 us
    pallas_call x1, Pallas kernels: 73.5 us -> 59.3 us  [local(): pl.pallas_call(functools.partial(kernel, nrow, ncol, bj, bk), out_shape=j...]
    another operation x11 -> x0, local copies, waits for them, and re-layouts: 2.25 us -> none  [parameters(): jnp.stack([ta, tb, scale(a, ta, nj), -scale(b, tb, nj), scale(a, ta, nk),...]
    another operation x3 -> x0, other arithmetic: 1.44 us -> none  [parameters(): jnp.stack([ta, tb, scale(a, ta, nj), -scale(b, tb, nj), scale(a, ta, nk),...]
where the time goes in v2:
time: 62.2 us; the launch traced here: 62.1 us
  Pallas kernels  59.3 us (95%)
  local copies, waits for them, and re-layouts  2.77 us (4%)
    pallas_call x1, Pallas kernels, local(): pl.pallas_call(functools.partial(kernel, nrow, ncol, bj, bk), out_shape=j...  59.3 us
    unnamed x1, local copies, waits for them, and re-layouts  2.77 us

profile of v2, /device:TPU:0, one launch (start us, length us, event | category | flops | bytes accessed | tf_op | source)
XLA Modules:
  0.0 62.1 jit_solution(1632473845389979469)
XLA Ops:
  0.0 59.3 %shard_map.100 = f32[6,128,512]{2,1,0:T(8,128)} custom-call(f32[6,128,512]{2,1,0:T(8,128)} %bitcast.6, f32[128,512]{1,0:T(8,128)} %bitcast.7, f32[6]{0:T(128)} %step_ref.1, s32[1,32]{1,0:T(1,128)} %count_ref.1, s32[1,1024]{1,0:T(1,128)} %bitcast.8, f32[3,1024]{1,0:T(4,128)} %frac_ref.1, s32[1,1024]{1,0:T(1,128)} %bitcast.9, ...), custom_call_target="tpu_custom_call" | custom-call | tf_op jit(solution)/shard_map/pallas_call | solution.py:399
  59.3 2.8 %copy.12 = f32[6,8,16,512]{3,2,1,0:T(8,128)} copy(f32[6,8,16,512]{3,2,1,0:T(8,128)} %bitcast.5) | data formatting | bytes 3145728

commit v3 on v2

--- a/solution.py
+++ b/solution.py
@@ -226,6 +226,86 @@
         def _(buffer=buffer):
             buffer[...] = jnp.zeros_like(buffer)
 
+    def solve_l(ref):
+        count = ref.shape[1]
+        for g in (0, 1):
+            vs = pl.ds(g * half_v, half_v)
+            wave = dot_split(ref[vs].reshape(half_v * count, bl), sh_ref[...], sl_ref[...])
+            wave = (wave.reshape(half_v, count, bl) * inv_ref[vs]).reshape(half_v * count, bl)
+            ref[vs] = dot_split(wave, sh_ref[...], sl_ref[...]).reshape(half_v, count, bl)
+
+    def chain(position, count, place_of, half, own, arrive, send, s_sem, r_sem, alpha, meanwhile):
+        def hop(side, v):
+            target = place_of(position + (1 if side == 0 else -1))
+            return pltpu.make_async_remote_copy(
+                src_ref=send.at[side, v], dst_ref=arrive.at[v, pl.ds(side * half, half)],
+                send_sem=s_sem.at[side, v], recv_sem=r_sem.at[side, v], device_id=target, device_id_type=MESH,
+            )
+
+        has_in = (position > 0, position < count - 1)
+        has_out = (position < count - 1, position > 0)
+
+        def head(v):
+            for side in (0, 1):
+
+                @pl.when(has_out[side] & jnp.logical_not(has_in[side]))
+                def _(side=side):
+                    send[side, v] = own[v, pl.ds(side * half, half), :]
+                    hop(side, v).start()
+
+        def pass_on(side):
+            @pl.when(jnp.logical_not(has_in[side]))
+            def _():
+                arrive[:, pl.ds(side * half, half), :] = jnp.zeros((nv, half, bl), F32)
+
+            @pl.when(has_in[side])
+            def _():
+                @pl.loop(0, nv)
+                def _(v):
+                    hop(side, v).wait_recv()
+
+                    @pl.when(has_out[side])
+                    def _():
+                        came = arrive[v, pl.ds(side * half, half), :]
+                        factor = jnp.where(
+                            iota((half, bl), 0) < half // 2,
+                            par_ref[v, alpha : alpha + 1, 0:1],
+                            par_ref[v, alpha + 1 : alpha + 2, 0:1],
+                        )
+                        send[side, v] = own[v, pl.ds(side * half, half), :] + factor * came
+                        hop(side, v).start()
+
+        def run():
+            lower = position < count // 2
+            upper = jnp.logical_not(lower)
+            inner = (position >= count // 4) & (position < count - count // 4)
+            pl.when(inner)(meanwhile)
+            pl.when(lower)(lambda: pass_on(0))
+            pl.when(upper)(lambda: pass_on(1))
+            pl.when(jnp.logical_not(inner))(meanwhile)
+            pl.when(lower)(lambda: pass_on(1))
+            pl.when(upper)(lambda: pass_on(0))
+
+        def finish():
+            for side in (0, 1):
+
+                @pl.when(has_out[side])
+                def _(side=side):
+                    @pl.loop(0, nv)
+                    def _(v):
+                        hop(side, v).wait_send()
+
+        return head, run, finish
+
+    def local_j():
+        solve_l(upd_ref)
+
+        @pl.loop(0, nv)
+        def _(v):
+            upd_ref[v] = dot3(gj[v], upd_ref[v])
+
+    head_j, run_j, finish_j = chain(r, nrow, lambda p: (p, c), 2 * bk, own_j, in_j, snd_j, j_send, j_recv, 7, local_j)
+
     lane = iota((rows, bl), 1)
     k_of = iota((rows, bl), 0) & (bk - 1)
 
@@ -247,73 +327,9 @@
             u = step_ref[v] * (spec_ref[...] * (total - 6.0 * f))
             upd_ref[v] = u
             own_j[v] = dot3(wj[v], u)
-
-    def solve_l(ref):
-        count = ref.shape[1]
-        for g in (0, 1):
-            vs = pl.ds(g * half_v, half_v)
-            wave = dot_split(ref[vs].reshape(half_v * count, bl), sh_ref[...], sl_ref[...])
-            wave = (wave.reshape(half_v, count, bl) * inv_ref[vs]).reshape(half_v * count, bl)
-            ref[vs] = dot_split(wave, sh_ref[...], sl_ref[...]).reshape(half_v, count, bl)
-
-    def chain(position, count, place_of, half, own, arrive, send, s_sem, r_sem, alpha, meanwhile):
-        def hop(side, v):
-            target = place_of(position + (1 if side == 0 else -1))
-            return pltpu.make_async_remote_copy(
-                src_ref=send.at[side, v], dst_ref=arrive.at[v, pl.ds(side * half, half)],
-                send_sem=s_sem.at[side, v], recv_sem=r_sem.at[side, v], device_id=target, device_id_type=MESH,
-            )
-
-        has_in = (position > 0, position < count - 1)
-        has_out = (position < count - 1, position > 0)
-
-        def pass_on(side):
-            @pl.when(jnp.logical_not(has_in[side]))
-            def _():
-                arrive[:, pl.ds(side * half, half), :] = jnp.zeros((nv, half, bl), F32)
-
-            @pl.loop(0, nv)
-            def _(v):
-                pl.when(has_in[side])(lambda: hop(side, v).wait_recv())
-
-                @pl.when(has_out[side])
-                def _():
-                    came = arrive[v, pl.ds(side * half, half), :]
-                    factor = jnp.where(
-                        iota((half, bl), 0) < half // 2, par_ref[v, alpha : alpha + 1, 0:1], par_ref[v, alpha + 1 : alpha + 2, 0:1]
-                    )
-                    send[side, v] = own[v, pl.ds(side * half, half), :] + factor * came
-                    hop(side, v).start()
-
-        lower = position < count // 2
-        upper = jnp.logical_not(lower)
-        inner = (position >= count // 4) & (position < count - count // 4)
-        pl.when(inner)(meanwhile)
-        pl.when(lower)(lambda: pass_on(0))
-        pl.when(upper)(lambda: pass_on(1))
-        pl.when(jnp.logical_not(inner))(meanwhile)
-        pl.when(lower)(lambda: pass_on(1))
-        pl.when(upper)(lambda: pass_on(0))
-
-        def finish():
-            for side in (0, 1):
-
-                @pl.when(has_out[side])
-                def _(side=side):
-                    @pl.loop(0, nv)
-                    def _(v):
-                        hop(side, v).wait_send()
-
-        return finish
-
-    def local_j():
-        solve_l(upd_ref)
-
-        @pl.loop(0, nv)
-        def _(v):
-            upd_ref[v] = dot3(gj[v], upd_ref[v])
-
-    finish_j = chain(r, nrow, lambda p: (p, c), 2 * bk, own_j, in_j, snd_j, j_send, j_recv, 7, local_j)
+            head_j(v)
+
+    run_j()
 
     for g in (0, 1):
         vs = pl.ds(g * half_v, half_v)
@@ -321,18 +337,21 @@
         wave = (wave.reshape(half_v, 4 * bk, bl) * inv_ref[vs]).reshape(half_v * 4 * bk, bl)
         own_j[vs] = dot_split(wave, sh_ref[...], sl_ref[...]).reshape(half_v, 4 * bk, bl)
 
+    def local_k():
+        @pl.loop(0, nv)
+        def _(v):
+            out_ref[v] = dot3(gk[v], upd_ref[v])
+
+    head_k, run_k, finish_k = chain(c, ncol, lambda p: (r, p), 2 * bj, own_k, in_k, snd_k, k_send, k_recv, 9, local_k)
+
     @pl.loop(0, nv)
     def _(v):
         y = upd_ref[v] + dot3(uj[v], own_j[v])
         upd_ref[v] = y
         own_k[v] = dot3(wk[v], y)
-
-    def local_k():
-        @pl.loop(0, nv)
-        def _(v):
-            out_ref[v] = dot3(gk[v], upd_ref[v])
-
-    finish_k = chain(c, ncol, lambda p: (r, p), 2 * bj, own_k, in_k, snd_k, k_send, k_recv, 9, local_k)
+        head_k(v)
+
+    run_k()
 
     @pl.loop(0, nv)
     def _(v):

time: 62.2 us -> 60.5 us (0.973)
  Pallas kernels: 59.3 us -> 57.6 us
    pallas_call x1, Pallas kernels: 59.3 us -> 57.6 us  [local(): pl.pallas_call(functools.partial(kernel, nrow, ncol, bj, bk), out_shape=j...]
where the time goes in v3:
time: 60.5 us; the launch traced here: 60.3 us
  Pallas kernels  57.6 us (95%)
  local copies, waits for them, and re-layouts  2.77 us (5%)
    pallas_call x1, Pallas kernels, local(): pl.pallas_call(functools.partial(kernel, nrow, ncol, bj, bk), out_shape=j...  57.6 us
    unnamed x1, local copies, waits for them, and re-layouts  2.77 us

profile of v3, /device:TPU:0, one launch (start us, length us, event | category | flops | bytes accessed | tf_op | source)
XLA Modules:
  0.0 60.3 jit_solution(16583753429205199689)
XLA Ops:
  0.0 57.6 %shard_map.100 = f32[6,128,512]{2,1,0:T(8,128)} custom-call(f32[6,128,512]{2,1,0:T(8,128)} %bitcast.6, f32[128,512]{1,0:T(8,128)} %bitcast.7, f32[6]{0:T(128)} %step_ref.1, s32[1,32]{1,0:T(1,128)} %count_ref.1, s32[1,1024]{1,0:T(1,128)} %bitcast.8, f32[3,1024]{1,0:T(4,128)} %frac_ref.1, s32[1,1024]{1,0:T(1,128)} %bitcast.9, ...), custom_call_target="tpu_custom_call" | custom-call | tf_op jit(solution)/shard_map/pallas_call | solution.py:418
  57.6 2.8 %copy.12 = f32[6,8,16,512]{3,2,1,0:T(8,128)} copy(f32[6,8,16,512]{3,2,1,0:T(8,128)} %bitcast.5) | data formatting | bytes 3145728
